TPU v7x, 256 devices: a whole 4x4x8 slice. The times are simulated.
256 devices in a mesh: rad: 8 (over y, x_hi), azi: 32 (over x_lo, z, core).
Axes of the slice: x: 4 (x_hi: 2, x_lo: 2; x = x_hi * 2 + x_lo), y: 4, z: 8, core: 2. Of those that a mesh axis runs over, the one named last changes fastest.
Arguments:
- density: float32 [256, 8192, 128], P('rad', 'azi'), may hold values from 0.1 to 2
- shift_cells: int32 [256], P('rad'), may hold values from 0 to 8191
- upwind_flags: int32 [256], P('rad'), may hold values 0 or 1
- courant: float32 [256, 128], P('rad'), may hold values from 0.05 to 0.9
- gain_factors: float32 [8, 128, 128], replicated, may hold values from -0.5 to 0.5
- rate_left: float32 [8, 128], replicated, may hold values from 0.1 to 1
- rate_right: float32 [8, 128], replicated, may hold values from -0.5 to 0.5
Outputs:
- evolved: float32 [256, 8192, 128], P('rad', 'azi')
All inputs are finite; a program needn't handle non-finite values. No bound on the sum of `upwind_flags` on one device may be relied on, other than what follows from the above.
Results may differ from a plain program's by a relative error of at most 0.0001.
Values sent between devices are 32-bit elements; how exact they have to be, the bound alone decides.
No kernel may reach another device: no remote copies, remote signals or barrier semaphores. Data moves between devices by JAX's collectives and lax.ppermute only.
A program may use at most 64 MiB of HBM per device.

v0:
```python
import jax
import jax.numpy as jnp
from jax import lax
from jax.sharding import PartitionSpec as P


def from_behind(shard, axis, by):
    length = lax.axis_size(axis)
    return lax.ppermute(shard, axis, [(i, (i + by) % length) for i in range(length)])


def extended(shard, sides, width):
    for axis, dim in sides:
        size, length = (lax.axis_size(axis), shard.shape[dim])
        up = [(i, (i + 1) % size) for i in range(size - 1)]
        down = [(j, i) for i, j in up]
        last = lax.slice_in_dim(shard, length - width, length, axis=dim)
        initial = lax.slice_in_dim(shard, 0, width, axis=dim)
        before = lax.ppermute(last, axis, up)
        after = lax.ppermute(initial, axis, down)
        shard = jnp.concatenate([before, shard, after], axis=dim)
    return shard


def window_row(row, start, length):
    return lax.dynamic_slice_in_dim(row, start, length, 0)


def coagulate(block, gain_factors, rate_left, rate_right):
    cells = block.reshape(-1, block.shape[-1])
    partner = jnp.dot(
        cells, rate_right.T, preferred_element_type=jnp.float32, precision=lax.Precision.HIGHEST
    )
    loss_rate = jnp.dot(
        partner, rate_left, preferred_element_type=jnp.float32, precision=lax.Precision.HIGHEST
    )
    gain = jnp.zeros_like(cells)
    for term in range(gain_factors.shape[0]):
        mapped = jnp.dot(
            cells,
            gain_factors[term],
            preferred_element_type=jnp.float32,
            precision=lax.Precision.HIGHEST,
        )
        gain = gain + partner[:, term : term + 1] * mapped
    result = cells + 0.25 * (gain - cells * loss_rate)
    return result.reshape(block.shape)


def shards(density, shift_cells, upwind_flags, courant, gain_factors, rate_left, rate_right):
    rows, width, bins = density.shape
    cycle_size = lax.axis_size("azi")
    whole_blocks = shift_cells // width
    within = shift_cells % width
    current = density
    for level in range((cycle_size - 1).bit_length()):
        moved = from_behind(current, "azi", 1 << level)
        taken = (whole_blocks >> level) % 2 == 1
        current = jnp.where(taken[:, None, None], moved, current)
    before = from_behind(current, "azi", 1)
    doubled = jnp.concatenate([before, current], axis=1)
    starts = width - within
    shifted = jax.vmap(lambda row, start: window_row(row, start, width))(doubled, starts)
    padded = extended(shifted, (("rad", 0),), 1)
    source = jnp.where((upwind_flags == 1)[:, None, None], padded[2:], padded[:-2])
    drifted = shifted - courant[:, None, :] * (shifted - source)
    return coagulate(drifted, gain_factors, rate_left, rate_right)


def solution(mesh):
    return jax.shard_map(
        shards,
        mesh=mesh,
        in_specs=(P("rad", "azi", None), P("rad"), P("rad"), P("rad", None), P(), P(), P()),
        out_specs=P("rad", "azi", None),
        check_vma=False,
    )
```

profile of v0, /device:TPU:56, one launch (start us, length us, event | category | flops | bytes accessed | tf_op | source)
XLA Modules:
  0.0 745.9 jit_solution(16982449957295653005)
XLA Ops:
  0.0 0.0 copy-start
  0.0 0.0 copy-start.2
  0.0 0.0 copy-start.6
  0.0 4.8 copy.8
  4.8 0.1 collective-permute-start
  4.9 0.0 copy-done.6
  4.9 47.9 %collective-permute-done = f32[32,256,128]{2,0,1:T(8,128)S(1)} collective-permute-done((f32[32,256,128]{2,0,1:T(8,128)S(1)}, f32[32,256,128]{2,0,1:T(8,128)S(1)}, u32[]{:S(2)}, u32[]{:S(2)}) %collective-permute-start) | collective-permute-done | bytes 4194336 | tf_op jit(solution)/shard_map/ppermute | solution.py:9
  52.8 0.0 copy-done.2
  52.8 2.5 broadcast_select_fusion
  55.3 2.0 collective-permute-start.1
  57.3 90.1 %collective-permute-done.1 = f32[32,256,128]{2,0,1:T(8,128)S(1)} collective-permute-done((f32[32,256,128]{2,0,1:T(8,128)S(1)}, f32[32,256,128]{2,0,1:T(8,128)S(1)}, u32[]{:S(2)}, u32[]{:S(2)}) %collective-permute-start.1) | collective-permute-done | bytes 4194336 | tf_op jit(solution)/shard_map/ppermute | solution.py:9
  147.4 1.1 broadcast_select_fusion.1
  148.5 4.6 collective-permute-start.2
  153.0 180.0 %collective-permute-done.2 = f32[32,256,128]{2,0,1:T(8,128)S(1)} collective-permute-done((f32[32,256,128]{2,0,1:T(8,128)S(1)}, f32[32,256,128]{2,0,1:T(8,128)S(1)}, u32[]{:S(2)}, u32[]{:S(2)}) %collective-permute-start.2) | collective-permute-done | bytes 4194336 | tf_op jit(solution)/shard_map/ppermute | solution.py:9
  333.0 1.1 broadcast_select_fusion.2
  334.1 3.6 collective-permute-start.3
  337.7 183.7 %collective-permute-done.3 = f32[32,256,128]{2,0,1:T(8,128)S(1)} collective-permute-done((f32[32,256,128]{2,0,1:T(8,128)S(1)}, f32[32,256,128]{2,0,1:T(8,128)S(1)}, u32[]{:S(2)}, u32[]{:S(2)}) %collective-permute-start.3) | collective-permute-done | bytes 4194336 | tf_op jit(solution)/shard_map/ppermute | solution.py:9
  521.4 1.1 broadcast_select_fusion.3
  522.5 2.8 collective-permute-start.4
  525.3 88.5 %collective-permute-done.4 = f32[32,256,128]{2,0,1:T(8,128)S(1)} collective-permute-done((f32[32,256,128]{2,0,1:T(8,128)S(1)}, f32[32,256,128]{2,0,1:T(8,128)S(1)}, u32[]{:S(2)}, u32[]{:S(2)}) %collective-permute-start.4) | collective-permute-done | bytes 4194336 | tf_op jit(solution)/shard_map/ppermute | solution.py:9
  613.7 1.1 broadcast_select_fusion.4
  614.8 0.1 collective-permute-start.5
  614.9 47.9 %collective-permute-done.5 = f32[32,256,128]{2,0,1:T(8,128)S(1)} collective-permute-done((f32[32,256,128]{2,0,1:T(8,128)S(1)}, f32[32,256,128]{2,0,1:T(8,128)S(1)}, u32[]{:S(2)}, u32[]{:S(2)}) %collective-permute-start.5) | collective-permute-done | bytes 4194336 | tf_op jit(solution)/shard_map/ppermute | solution.py:9
  662.8 4.2 pad_maximum_fusion
  667.0 0.0 copy-start.7
  667.0 0.0 copy-start.4
  667.0 10.1 %gather_fusion = f32[32,256,128]{2,0,1:T(8,128)} fusion(f32[32,512,128]{2,0,1:T(8,128)} %pad_maximum_fusion, s32[32]{0:T(128)S(1)} %fusion.41), kind=kCustom, calls=%fused_computation | custom fusion | bytes 8388992 | tf_op jit(solution)/shard_map/vmap()/gather | solution.py:26
  677.1 1.7 fusion.42
  678.9 5.0 collective-permute-start.6
  683.8 2.4 collective-permute-start.7
  686.2 0.0 copy-done.7
  686.3 1.3 collective-permute-done.6
  687.6 5.5 collective-permute-done.7
  693.1 0.0 copy-done.4
  693.1 6.7 fusion.13
  699.9 0.0 copy-start.5
  699.9 2.4 copy.10
  702.3 0.0 copy-done.5
  702.3 3.6 fusion.44
  706.0 0.2 fusion.43
  706.1 0.0 copy-done
  706.2 0.0 copy-start.3
  706.2 6.9 convolution_multiply_fusion
  713.0 0.0 copy-done.3
  713.0 3.6 convolution_multiply_fusion.8
  716.7 3.8 fusion.9
  720.5 3.7 fusion.8
  724.2 4.0 fusion.7
  728.2 3.7 fusion.6
  731.9 3.8 fusion.5
  735.7 4.0 fusion.4
  739.7 0.0 copy-start.1
  739.7 5.7 fusion.3
  745.4 0.0 copy-done.1
  (4 shorter events, 0.1 us)
Async XLA Ops:
  0.0 706.1 %copy-start = (f32[8,128]{1,0:T(8,128)S(1)}, f32[8,128]{1,0:T(8,128)}, u32[]{:S(2)}) copy-start(f32[8,128]{1,0:T(8,128)} %param.12) | copy-start | bytes 12292
  0.0 52.8 %copy-start.2 = (f32[32,256,128]{2,1,0:T(8,128)S(1)}, f32[32,256,128]{2,1,0:T(8,128)}, u32[]{:S(2)}) copy-start(f32[32,256,128]{2,1,0:T(8,128)} %param.7) | copy-start | bytes 12582916
  0.0 4.9 copy-start.6
  4.8 48.0 %collective-permute-start = (f32[32,256,128]{2,0,1:T(8,128)S(1)}, f32[32,256,128]{2,0,1:T(8,128)S(1)}, u32[]{:S(2)}, u32[]{:S(2)}) collective-permute-start(f32[32,256,128]{2,0,1:T(8,128)S(1)} %copy.8), channel_id=1, source_target_pairs={{0,1},{1,2},{2,3},{3,4},{4,5},{5,6},{6,7},{7,8},{8,9},{9,10},{10,1... | collective-permute-start | bytes 12582920 | tf_op jit(solution)/shard_map/ppermute | solution.py:9
  55.3 92.1 %collective-permute-start.1 = (f32[32,256,128]{2,0,1:T(8,128)S(1)}, f32[32,256,128]{2,0,1:T(8,128)S(1)}, u32[]{:S(2)}, u32[]{:S(2)}) collective-permute-start(f32[32,256,128]{2,0,1:T(8,128)S(1)} %broadcast_select_fusion), channel_id=1, source_target_pairs={{0,2},{1,3},{2,4},{3,5},{4,6},{5,7},{6,8},{7,9},{8,10},{9,11},{10,... | collective-permute-start | bytes 12582920 | tf_op jit(solution)/shard_map/ppermute | solution.py:9
  148.5 184.5 %collective-permute-start.2 = (f32[32,256,128]{2,0,1:T(8,128)S(1)}, f32[32,256,128]{2,0,1:T(8,128)S(1)}, u32[]{:S(2)}, u32[]{:S(2)}) collective-permute-start(f32[32,256,128]{2,0,1:T(8,128)S(1)} %broadcast_select_fusion.1), channel_id=1, source_target_pairs={{0,4},{1,5},{2,6},{3,7},{4,8},{5,9},{6,10},{7,11},{8,12},{9,13},{1... | collective-permute-start | bytes 12582920 | tf_op jit(solution)/shard_map/ppermute | solution.py:9
  334.1 187.3 %collective-permute-start.3 = (f32[32,256,128]{2,0,1:T(8,128)S(1)}, f32[32,256,128]{2,0,1:T(8,128)S(1)}, u32[]{:S(2)}, u32[]{:S(2)}) collective-permute-start(f32[32,256,128]{2,0,1:T(8,128)S(1)} %broadcast_select_fusion.2), channel_id=1, source_target_pairs={{0,8},{1,9},{2,10},{3,11},{4,12},{5,13},{6,14},{7,15},{8,16},{9,17... | collective-permute-start | bytes 12582920 | tf_op jit(solution)/shard_map/ppermute | solution.py:9
  522.5 91.2 %collective-permute-start.4 = (f32[32,256,128]{2,0,1:T(8,128)S(1)}, f32[32,256,128]{2,0,1:T(8,128)S(1)}, u32[]{:S(2)}, u32[]{:S(2)}) collective-permute-start(f32[32,256,128]{2,0,1:T(8,128)S(1)} %broadcast_select_fusion.3), channel_id=1, source_target_pairs={{0,16},{1,17},{2,18},{3,19},{4,20},{5,21},{6,22},{7,23},{8,24},{9,... | collective-permute-start | bytes 12582920 | tf_op jit(solution)/shard_map/ppermute | solution.py:9
  614.8 48.0 %collective-permute-start.5 = (f32[32,256,128]{2,0,1:T(8,128)S(1)}, f32[32,256,128]{2,0,1:T(8,128)S(1)}, u32[]{:S(2)}, u32[]{:S(2)}) collective-permute-start(f32[32,256,128]{2,0,1:T(8,128)S(1)} %broadcast_select_fusion.4), channel_id=1, source_target_pairs={{0,1},{1,2},{2,3},{3,4},{4,5},{5,6},{6,7},{7,8},{8,9},{9,10},{10,1... | collective-permute-start | bytes 12582920 | tf_op jit(solution)/shard_map/ppermute | solution.py:9
  667.0 19.2 %copy-start.7 = (s32[32]{0:T(128)S(1)}, s32[32]{0:T(128)}, u32[]{:S(2)}) copy-start(s32[32]{0:T(128)} %param.9) | copy-start | bytes 388
  667.0 26.1 %copy-start.4 = (f32[32,128]{1,0:T(8,128)S(1)}, f32[32,128]{1,0:T(8,128)}, u32[]{:S(2)}) copy-start(f32[32,128]{1,0:T(8,128)} %param.10) | copy-start | bytes 49156
  678.9 8.7 %collective-permute-start.6 = (f32[1,256,128]{2,0,1:T(1,128)S(1)}, f32[1,256,128]{2,0,1:T(1,128)S(1)}, u32[]{:S(2)}, u32[]{:S(2)}) collective-permute-start(f32[1,256,128]{2,0,1:T(1,128)S(1)} %get-tuple-element.7), channel_id=1, source_target_pairs={{32,0},{64,32},{96,64},{128,96},{160,128},{192,160},{224,192},{33,... | collective-permute-start | bytes 393224 | tf_op jit(solution)/shard_map/ppermute | solution.py:20
  683.8 9.3 %collective-permute-start.7 = (f32[1,256,128]{2,0,1:T(1,128)S(1)}, f32[1,256,128]{2,0,1:T(1,128)S(1)}, u32[]{:S(2)}, u32[]{:S(2)}) collective-permute-start(f32[1,256,128]{2,0,1:T(1,128)S(1)} %get-tuple-element.8), channel_id=1, source_target_pairs={{0,32},{32,64},{64,96},{96,128},{128,160},{160,192},{192,224},{1,3... | collective-permute-start | bytes 393224 | tf_op jit(solution)/shard_map/ppermute | solution.py:19
  699.9 2.5 copy-start.5
  706.2 6.9 copy-start.3
  739.7 5.7 copy-start.1
where the time goes:
time: 754 us; the launch traced here: 746 us
  waiting for transfers between devices  645 us (86%)
  matrix products  42.8 us (6%)
  starting transfers between devices  20.5 us (3%)
  local copies, waits for them, and re-layouts  19.3 us (3%)
  other arithmetic  17.8 us (2%)
    ppermute x6, waiting for transfers between devices, from_behind(): lax.ppermute(shard, axis, [(i, (i + by) % length) for i in range(length)])  638 us
    dot_general x8, matrix products, coagulate(): jnp.dot(cells, gain_factors[term], preferred_element_type=jnp.float32, pr...  32.3 us
  transfers between devices with their start and end apart: 8, of which 8 were waited for; matrix products, arithmetic and copies ran while one was open for 0% of the time, Pallas kernels for 0%

commit v1 on v0

v1 whole, which is shorter than its diff:
```python
import functools

import jax
import jax.numpy as jnp
from jax import lax
from jax.experimental import pallas as pl
from jax.experimental.pallas import tpu as pltpu
from jax.sharding import PartitionSpec as P

MIB = 2**20


def roll_kernel(shift_ref, row_ref, out_ref, sem):
    cells = row_ref.shape[0]
    shift = shift_ref[0]

    @pl.when(shift > 0)
    def _():
        pltpu.make_async_copy(row_ref.at[pl.ds(cells - shift, shift)], out_ref.at[pl.ds(0, shift)], sem).start()

    pltpu.make_async_copy(row_ref.at[pl.ds(0, cells - shift)], out_ref.at[pl.ds(shift, cells - shift)], sem).start()
    pltpu.make_async_copy(row_ref, out_ref, sem).wait()


def rolled(row, shift):
    cells, bins = row.shape
    out = pl.pallas_call(
        roll_kernel,
        out_shape=jax.ShapeDtypeStruct((cells, 1, bins), row.dtype),
        in_specs=[pl.BlockSpec(memory_space=pltpu.SMEM), pl.BlockSpec(memory_space=pl.ANY)],
        out_specs=pl.BlockSpec(memory_space=pl.ANY),
        scratch_shapes=[pltpu.SemaphoreType.DMA],
        compiler_params=pltpu.CompilerParams(vmem_limit_bytes=16 * MIB),
        cost_estimate=pl.CostEstimate(flops=0, bytes_accessed=8 * cells * bins, transcendentals=0),
        name="roll",
    )(shift, row.reshape(cells, 1, bins))
    return out.reshape(cells, bins)


def split(x):
    high = x.astype(jnp.bfloat16)
    return high, (x - high.astype(jnp.float32)).astype(jnp.bfloat16)


def evolve_kernel(flags_ref, x_ref, before_ref, after_ref, courant_ref, gain_ref, left_ref, right_ref, out_ref,
                  upper_ref, lower_ref, cells_ref):
    rows, width, bins = x_ref.shape
    terms = gain_ref.shape[0]
    total = (terms + 1) * bins

    @pl.when(pl.program_id(0) == 0)
    def _():
        diagonal = lax.broadcasted_iota(jnp.int32, (bins, bins), 0) == lax.broadcasted_iota(jnp.int32, (bins, bins), 1)
        for p in range(terms):
            net = gain_ref[p] - jnp.where(diagonal, left_ref[p : p + 1, :], 0.0)
            high, low = split(0.25 * net)
            upper_ref[:bins, p * bins : (p + 1) * bins] = high
            upper_ref[bins:, p * bins : (p + 1) * bins] = high
            lower_ref[:, p * bins : (p + 1) * bins] = low
        high, low = split(right_ref[...])
        upper_ref[:bins, terms * bins : total] = high
        upper_ref[bins:, terms * bins : total] = high
        lower_ref[:, terms * bins : total] = low

    for r in range(rows):
        here = x_ref[r]
        larger = x_ref[r + 1] if r + 1 < rows else after_ref[0]
        smaller = x_ref[r - 1] if r > 0 else before_ref[0]
        source = jnp.where(flags_ref[r] == 1, larger, smaller)
        cells_ref[r * width : (r + 1) * width, :] = here - courant_ref[r : r + 1, :] * (here - source)

    chunk = min(256, rows * width)
    for start in range(0, rows * width, chunk):
        n = cells_ref[start : start + chunk, :]
        high, low = split(n)
        both = jnp.concatenate([high, low], axis=1)

        def product(first, last):
            return jnp.dot(both, upper_ref[:, first:last], preferred_element_type=jnp.float32) + jnp.dot(
                high, lower_ref[:, first:last], preferred_element_type=jnp.float32
            )

        partner = product(terms * bins, total)
        result = n
        for p in range(0, terms, 2):
            mapped = product(p * bins, (p + 2) * bins)
            result = result + partner[:, p : p + 1] * mapped[:, :bins] + partner[:, p + 1 : p + 2] * mapped[:, bins:]
        out_ref[start // width : (start + chunk) // width] = result.reshape(chunk // width, width, bins)


def evolved(shifted, before, after, upwind_flags, courant, gain_factors, rate_left, rate_right):
    rows, width, bins = shifted.shape
    terms = gain_factors.shape[0]
    step = 32
    right = jnp.zeros((bins, bins), jnp.float32).at[:, :terms].set(rate_right.T)
    whole = lambda *shape: pl.BlockSpec(shape, lambda i: (0,) * len(shape))
    return pl.pallas_call(
        evolve_kernel,
        grid=(width // step,),
        out_shape=jax.ShapeDtypeStruct(shifted.shape, shifted.dtype),
        in_specs=[
            pl.BlockSpec(memory_space=pltpu.SMEM),
            pl.BlockSpec((rows, step, bins), lambda i: (0, i, 0)),
            pl.BlockSpec((1, step, bins), lambda i: (0, i, 0)),
            pl.BlockSpec((1, step, bins), lambda i: (0, i, 0)),
            whole(rows, bins),
            whole(terms, bins, bins),
            whole(terms, bins),
            whole(bins, bins),
        ],
        out_specs=pl.BlockSpec((rows, step, bins), lambda i: (0, i, 0)),
        scratch_shapes=[
            pltpu.VMEM((2 * bins, (terms + 1) * bins), jnp.bfloat16),
            pltpu.VMEM((bins, (terms + 1) * bins), jnp.bfloat16),
            pltpu.VMEM((rows * step, bins), jnp.float32),
        ],
        compiler_params=pltpu.CompilerParams(vmem_limit_bytes=32 * MIB),
        name="evolve",
    )(upwind_flags, shifted, before, after, courant, gain_factors, rate_left, right)


def shards(density, shift_cells, upwind_flags, courant, gain_factors, rate_left, rate_right):
    rows, width, bins = density.shape
    ring, bands = lax.axis_size("azi"), lax.axis_size("rad")
    row = lax.all_to_all(density, "azi", 0, 0, tiled=True)
    shift = lax.dynamic_slice(shift_cells, (lax.axis_index("azi"),), (1,))
    row = rolled(row.reshape(ring * width, bins), shift)
    shifted = lax.all_to_all(row.reshape(ring, width, bins), "azi", 0, 0, tiled=True)
    up = [(i, i + 1) for i in range(bands - 1)]
    before = lax.ppermute(shifted[rows - 1 :], "rad", up)
    after = lax.ppermute(shifted[:1], "rad", [(j, i) for i, j in up])
    return evolved(shifted, before, after, upwind_flags, courant, gain_factors, rate_left, rate_right)


def solution(mesh):
    return jax.shard_map(
        shards,
        mesh=mesh,
        in_specs=(P("rad", "azi", None), P("rad"), P("rad"), P("rad", None), P(), P(), P()),
        out_specs=P("rad", "azi", None),
        check_vma=False,
    )
```

time: 754 us -> 244 us (0.32)
  waiting for transfers between devices: 645 us -> 192 us
  matrix products: 42.8 us -> 0 us
  Pallas kernels: 0 us -> 18.9 us
  other arithmetic: 17.8 us -> 1.23 us
  local copies, waits for them, and re-layouts: 19.3 us -> 3.71 us
    ppermute x8 -> x2, waiting for transfers between devices: 645 us -> 6 us  [the longest x1 5.71 us: shards(): before = lax.ppermute(shifted[rows - 1:], 'rad', up)]
    all_to_all x0 -> x2, waiting for transfers between devices: none -> 186 us  [the longest x1 93.1 us: shards(): row = lax.all_to_all(density, 'azi', 0, 0, tiled=True)]
    dot_general x10 -> x0, matrix products: 42.8 us -> none  [the longest x8 32.3 us: coagulate(): jnp.dot(cells, gain_factors[term], preferred_element_type=jnp.float32, pr...]
    pallas_call x0 -> x2, Pallas kernels: none -> 18.9 us  [the longest x1 16 us: evolved(): pl.pallas_call(evolve_kernel, grid=(width // step,), out_shape=jax.ShapeD...]
    all_to_all x0 -> x2, starting transfers between devices: none -> 18.2 us  [the longest x1 9.84 us: shards(): row = lax.all_to_all(density, 'azi', 0, 0, tiled=True)]
    ppermute x8 -> x2, starting transfers between devices: 20.5 us -> 7.35 us  [the longest x1 4.8 us: shards(): after = lax.ppermute(shifted[:1], 'rad', [(j, i) for i, j in up])]
    gather x1 -> x0, local copies, waits for them, and re-layouts: 10.1 us -> none  [window_row(): return lax.dynamic_slice_in_dim(row, start, length, 0)]
  transfers between devices with their start and end apart: 8 -> 4, of which waited for: 8 -> 4; matrix products, arithmetic and copies ran while one was open for 0% -> 1% of each run, Pallas kernels for 0% -> 0%
where the time goes in v1:
time: 244 us; the launch traced here: 242 us
  waiting for transfers between devices  192 us (79%)
  starting transfers between devices  25.5 us (10%)
  Pallas kernels  18.9 us (8%)
  local copies, waits for them, and re-layouts  3.71 us (2%)
    all_to_all x1, waiting for transfers between devices, shards(): row = lax.all_to_all(density, 'azi', 0, 0, tiled=True)  93.1 us
    all_to_all x1, waiting for transfers between devices, shards(): lax.all_to_all(row.reshape(ring, width, bins), 'azi', 0, 0, tiled=True)  93.1 us
    pallas_call x1, Pallas kernels, evolved(): pl.pallas_call(evolve_kernel, grid=(width // step,), out_shape=jax.ShapeD...  16 us
    all_to_all x1, starting transfers between devices, shards(): row = lax.all_to_all(density, 'azi', 0, 0, tiled=True)  9.84 us
    all_to_all x1, starting transfers between devices, shards(): lax.all_to_all(row.reshape(ring, width, bins), 'azi', 0, 0, tiled=True)  8.35 us
    ppermute x1, waiting for transfers between devices, shards(): before = lax.ppermute(shifted[rows - 1:], 'rad', up)  5.71 us
  transfers between devices with their start and end apart: 4, of which 4 were waited for; matrix products, arithmetic and copies ran while one was open for 1% of the time, Pallas kernels for 0%

profile of v1, /device:TPU:56, one launch (start us, length us, event | category | flops | bytes accessed | tf_op | source)
XLA Modules:
  0.0 241.7 jit_solution(1587311431128831078)
XLA Ops:
  0.0 0.0 copy-start.6
  0.0 9.8 %all-to-all-start = ((f32[32,256,128]{2,1,0:T(8,128)}), f32[32,256,128]{2,1,0:T(8,128)}, u32[]{:S(2)}, u32[]{:S(2)}) async-start(f32[32,256,128]{2,1,0:T(8,128)} %param.9), calls=%async_computation | async-start | bytes 8388608 | tf_op jit(solution)/shard_map/all_to_all | solution.py:125
  9.9 0.0 copy-done.6
  9.9 0.6 dynamic_slice.3.shift_ref
  10.5 93.1 %all-to-all-done = f32[32,256,128]{2,1,0:T(8,128)} async-done(((f32[32,256,128]{2,1,0:T(8,128)}), f32[32,256,128]{2,1,0:T(8,128)}, u32[]{:S(2)}, u32[]{:S(2)}) %all-to-all-start) | async-done | bytes 4194336 | tf_op jit(solution)/shard_map/all_to_all | solution.py:125
  103.6 2.9 %roll.1 = f32[8192,1,128]{2,1,0:T(1,128)S(1)} custom-call(s32[1]{0:T(128)} %dynamic_slice.3.shift_ref, f32[8192,1,128]{2,1,0:T(1,128)} %bitcast.row_ref), custom_call_target="tpu_custom_call" | custom-call | bytes 8388608 | tf_op jit(solution)/shard_map/roll/pallas_call | solution.py:27
  106.5 0.0 copy-start
  106.5 2.0 copy-done
  108.5 0.0 copy-start.5
  108.5 0.0 copy-start.1
  108.5 0.0 copy-start.2
  108.5 0.0 copy-start.3
  108.5 0.0 copy-start.4
  108.5 8.4 %all-to-all-start.1 = ((f32[32,256,128]{2,1,0:T(8,128)}), f32[32,256,128]{2,1,0:T(8,128)}, u32[]{:S(2)}, u32[]{:S(2)}) async-start(f32[32,256,128]{2,1,0:T(8,128)} %bitcast.3), calls=%async_computation.1 | async-start | bytes 8388608 | tf_op jit(solution)/shard_map/all_to_all | solution.py:128
  116.9 0.6 compare_reduce_fusion
  117.5 93.1 %all-to-all-done.1.x_ref = f32[32,256,128]{2,1,0:T(8,128)} async-done(((f32[32,256,128]{2,1,0:T(8,128)}), f32[32,256,128]{2,1,0:T(8,128)}, u32[]{:S(2)}, u32[]{:S(2)}) %all-to-all-start.1) | async-done | bytes 4194336 | tf_op jit(solution)/shard_map/all_to_all | solution.py:128
  210.6 1.0 fusion
  211.6 4.8 %collective-permute-start.1 = (f32[1,256,128]{2,1,0:T(8,128)S(1)}, f32[1,256,128]{2,1,0:T(8,128)S(1)}, u32[]{:S(2)}, u32[]{:S(2)}) collective-permute-start(f32[1,256,128]{2,1,0:T(8,128)S(1)} %get-tuple-element.17), channel_id=1, source_target_pairs={{32,0},{64,32},{96,64},{128,96},{160,128},{192,160},{224,192},{33,... | collective-permute-start | bytes 393224 | tf_op jit(solution)/shard_map/ppermute | solution.py:131
  216.4 2.5 %collective-permute-start = (f32[1,256,128]{2,1,0:T(8,128)S(1)}, f32[1,256,128]{2,1,0:T(8,128)S(1)}, u32[]{:S(2)}, u32[]{:S(2)}) collective-permute-start(f32[1,256,128]{2,1,0:T(8,128)S(1)} %get-tuple-element.18), channel_id=1, source_target_pairs={{0,32},{32,64},{64,96},{96,128},{128,160},{160,192},{192,224},{1,3... | collective-permute-start | bytes 393224 | tf_op jit(solution)/shard_map/ppermute | solution.py:130
  219.0 0.0 copy-done.5
  219.0 0.6 broadcast_select_fusion
  219.5 0.1 copy.11
  219.7 0.3 collective-permute-done.1.after_ref
  220.0 5.7 %collective-permute-done.before_ref = f32[1,256,128]{2,1,0:T(8,128)S(1)} collective-permute-done((f32[1,256,128]{2,1,0:T(8,128)S(1)}, f32[1,256,128]{2,1,0:T(8,128)S(1)}, u32[]{:S(2)}, u32[]{:S(2)}) %collective-permute-start) | collective-permute-done | bytes 131104 | tf_op jit(solution)/shard_map/ppermute | solution.py:130
  225.7 0.0 copy-done.1
  225.7 0.0 copy-done.2
  225.7 0.0 copy-done.3
  225.7 0.0 copy-done.4
  225.7 16.0 %evolve.1 = f32[32,256,128]{2,1,0:T(8,128)} custom-call(s32[32]{0:T(128)S(1)} %copy-done.4, f32[32,256,128]{2,1,0:T(8,128)} %all-to-all-done.1.x_ref, f32[1,256,128]{2,1,0:T(8,128)S(1)} %collective-permute-done.before_ref, f32[1,256,128]{2,1,0:T(8,128)S(1)} %collective-permute-done.1.after_ref, f32[32,128]{1,0:T(8,128)S(1)} %copy-done.2, ...), custom_call_target="tpu_custom_call" | custom-call | tf_op jit(solution)/shard_map/evolve/pallas_call | solution.py:97
  (1 shorter events, 0.0 us)
Async XLA Ops:
  0.0 9.9 %copy-start.6 = (s32[32]{0:T(128)S(1)}, s32[32]{0:T(128)}, u32[]{:S(2)}) copy-start(s32[32]{0:T(128)} %param.10) | copy-start | bytes 388
  0.0 103.6 %all-to-all-start = ((f32[32,256,128]{2,1,0:T(8,128)}), f32[32,256,128]{2,1,0:T(8,128)}, u32[]{:S(2)}, u32[]{:S(2)}) async-start(f32[32,256,128]{2,1,0:T(8,128)} %param.9), calls=%async_computation | async-start | bytes 8388608 | tf_op jit(solution)/shard_map/all_to_all | solution.py:125
  106.5 2.0 copy-start
  108.5 110.5 %copy-start.5 = (f32[8,128]{1,0:T(8,128)S(1)}, f32[8,128]{1,0:T(8,128)}, u32[]{:S(2)}) copy-start(f32[8,128]{1,0:T(8,128)} %param.15) | copy-start | bytes 12292
  108.5 117.2 %copy-start.1 = (f32[8,128,128]{2,1,0:T(8,128)S(1)}, f32[8,128,128]{2,1,0:T(8,128)}, u32[]{:S(2)}) copy-start(f32[8,128,128]{2,1,0:T(8,128)} %gain_ref.1) | copy-start | bytes 1572868
  108.5 117.2 %copy-start.2 = (f32[32,128]{1,0:T(8,128)S(1)}, f32[32,128]{1,0:T(8,128)}, u32[]{:S(2)}) copy-start(f32[32,128]{1,0:T(8,128)} %courant_ref.1) | copy-start | bytes 49156
  108.5 117.2 %copy-start.3 = (f32[8,128]{1,0:T(8,128)S(1)}, f32[8,128]{1,0:T(8,128)}, u32[]{:S(2)}) copy-start(f32[8,128]{1,0:T(8,128)} %left_ref.1) | copy-start | bytes 12292
  108.5 117.2 %copy-start.4 = (s32[32]{0:T(128)S(1)}, s32[32]{0:T(128)}, u32[]{:S(2)}) copy-start(s32[32]{0:T(128)} %flags_ref.1) | copy-start | bytes 388
  108.5 102.1 %all-to-all-start.1 = ((f32[32,256,128]{2,1,0:T(8,128)}), f32[32,256,128]{2,1,0:T(8,128)}, u32[]{:S(2)}, u32[]{:S(2)}) async-start(f32[32,256,128]{2,1,0:T(8,128)} %bitcast.3), calls=%async_computation.1 | async-start | bytes 8388608 | tf_op jit(solution)/shard_map/all_to_all | solution.py:128
  211.6 8.4 %collective-permute-start.1 = (f32[1,256,128]{2,1,0:T(8,128)S(1)}, f32[1,256,128]{2,1,0:T(8,128)S(1)}, u32[]{:S(2)}, u32[]{:S(2)}) collective-permute-start(f32[1,256,128]{2,1,0:T(8,128)S(1)} %get-tuple-element.17), channel_id=1, source_target_pairs={{32,0},{64,32},{96,64},{128,96},{160,128},{192,160},{224,192},{33,... | collective-permute-start | bytes 393224 | tf_op jit(solution)/shard_map/ppermute | solution.py:131
  216.4 9.3 %collective-permute-start = (f32[1,256,128]{2,1,0:T(8,128)S(1)}, f32[1,256,128]{2,1,0:T(8,128)S(1)}, u32[]{:S(2)}, u32[]{:S(2)}) collective-permute-start(f32[1,256,128]{2,1,0:T(8,128)S(1)} %get-tuple-element.18), channel_id=1, source_target_pairs={{0,32},{32,64},{64,96},{96,128},{128,160},{160,192},{192,224},{1,3... | collective-permute-start | bytes 393224 | tf_op jit(solution)/shard_map/ppermute | solution.py:130

commit v2 on v1

v2 whole, which is shorter than its diff:
```python
import jax
import jax.numpy as jnp
from jax import lax
from jax.experimental import pallas as pl
from jax.experimental.pallas import tpu as pltpu
from jax.sharding import PartitionSpec as P

MIB = 2**20


def roll_kernel(shift_ref, row_ref, out_ref, held_ref, in_sems, out_sem):
    cells = row_ref.shape[0]
    parts = in_sems.shape[0]
    size = cells // parts
    shift = shift_ref[0]
    loads = [
        pltpu.make_async_copy(row_ref.at[pl.ds(k * size, size)], held_ref.at[pl.ds(k * size, size)], in_sems.at[k])
        for k in range(parts)
    ]
    for load in loads:
        load.start()
    for k in range(parts):
        loads[k].wait()
        at = lax.rem(k * size + shift, cells)
        first = jnp.minimum(size, cells - at)
        pltpu.make_async_copy(held_ref.at[pl.ds(k * size, first)], out_ref.at[pl.ds(at, first)], out_sem).start()

        @pl.when(first < size)
        def _():
            rest = size - first
            pltpu.make_async_copy(held_ref.at[pl.ds(k * size + first, rest)], out_ref.at[pl.ds(0, rest)], out_sem).start()

    pltpu.make_async_copy(held_ref, out_ref, out_sem).wait()


def rolled(row, shift):
    cells, bins = row.shape
    parts = 2
    out = pl.pallas_call(
        roll_kernel,
        out_shape=jax.ShapeDtypeStruct((cells, 1, bins), row.dtype),
        in_specs=[pl.BlockSpec(memory_space=pltpu.SMEM), pl.BlockSpec(memory_space=pl.ANY)],
        out_specs=pl.BlockSpec(memory_space=pltpu.HBM),
        scratch_shapes=[
            pltpu.VMEM((cells, 1, bins), row.dtype),
            pltpu.SemaphoreType.DMA((parts,)),
            pltpu.SemaphoreType.DMA,
        ],
        compiler_params=pltpu.CompilerParams(vmem_limit_bytes=16 * MIB),
        cost_estimate=pl.CostEstimate(flops=0, bytes_accessed=8 * cells * bins, transcendentals=0),
        name="roll",
    )(shift, row.reshape(cells, 1, bins))
    return out.reshape(cells, bins)


def split(x):
    high = x.astype(jnp.bfloat16)
    return high, (x - high.astype(jnp.float32)).astype(jnp.bfloat16)


def weights_kernel(gain_ref, left_ref, right_ref, upper_ref, lower_ref):
    terms, bins, _ = gain_ref.shape
    diagonal = lax.broadcasted_iota(jnp.int32, (bins, bins), 0) == lax.broadcasted_iota(jnp.int32, (bins, bins), 1)
    for p in range(terms):
        high, low = split(0.25 * (gain_ref[p] - jnp.where(diagonal, left_ref[p : p + 1, :], 0.0)))
        columns = slice(p * bins, (p + 1) * bins)
        upper_ref[:bins, columns] = high
        upper_ref[bins:, columns] = high
        lower_ref[:, columns] = low
    right = right_ref[...]
    right = jnp.concatenate([right, right, jnp.zeros((bins - 2 * terms, bins), jnp.float32)], axis=0).T
    high, low = split(right)
    first = lax.broadcasted_iota(jnp.int32, (bins, bins), 1) < terms
    high, low = high.astype(jnp.float32), low.astype(jnp.float32)
    upper_ref[:bins, terms * bins :] = jnp.where(first, high, low).astype(jnp.bfloat16)
    upper_ref[bins:, terms * bins :] = jnp.where(first, high, 0.0).astype(jnp.bfloat16)


def weights(gain_factors, rate_left, rate_right):
    terms, bins, _ = gain_factors.shape
    vmem = pl.BlockSpec(memory_space=pltpu.VMEM)
    return pl.pallas_call(
        weights_kernel,
        out_shape=(
            jax.ShapeDtypeStruct((2 * bins, (terms + 1) * bins), jnp.bfloat16),
            jax.ShapeDtypeStruct((bins, terms * bins), jnp.bfloat16),
        ),
        in_specs=[vmem] * 3,
        out_specs=(vmem, vmem),
        cost_estimate=pl.CostEstimate(flops=0, bytes_accessed=2 * MIB, transcendentals=0),
        name="weights",
    )(gain_factors, rate_left, rate_right)


def coagulated(n, upper_ref, lower_ref):
    bins = n.shape[1]
    terms = lower_ref.shape[1] // bins
    high, low = split(n)
    both = jnp.concatenate([high, low], axis=1)
    partner = jnp.dot(both, upper_ref[:, terms * bins :], preferred_element_type=jnp.float32)
    partner = partner + pltpu.roll(partner, bins - terms, 1)
    result = n
    for p in range(0, terms, 2):
        columns = slice(p * bins, (p + 2) * bins)
        mapped = jnp.dot(both, upper_ref[:, columns], preferred_element_type=jnp.float32) + jnp.dot(
            high, lower_ref[:, columns], preferred_element_type=jnp.float32
        )
        result = result + partner[:, p : p + 1] * mapped[:, :bins] + partner[:, p + 1 : p + 2] * mapped[:, bins:]
    return result


def drifted(here, larger, smaller, flag, courant):
    return here - courant * (here - jnp.where(flag == 1, larger, smaller))


def interior_kernel(flags_ref, x_ref, courant_ref, upper_ref, lower_ref, out_ref, cells_ref):
    rows, width, bins = x_ref.shape
    for r in range(1, rows - 1):
        cells_ref[(r - 1) * width : r * width, :] = drifted(
            x_ref[r], x_ref[r + 1], x_ref[r - 1], flags_ref[r], courant_ref[r : r + 1, :]
        )
    result = coagulated(cells_ref[...], upper_ref, lower_ref)
    out_ref[1 : rows - 1] = result.reshape(rows - 2, width, bins)


def ends_kernel(flags_ref, low_ref, high_ref, before_ref, after_ref, courant_ref, upper_ref, lower_ref, kept_ref,
                out_ref, cells_ref, sems):
    del kept_ref
    width = low_ref.shape[1]
    rows = flags_ref.shape[0]
    cells_ref[:width, :] = drifted(low_ref[0], low_ref[1], before_ref[0], flags_ref[0], courant_ref[:1, :])
    cells_ref[width:, :] = drifted(high_ref[1], after_ref[0], high_ref[0], flags_ref[rows - 1], courant_ref[rows - 1 :, :])
    cells_ref[...] = coagulated(cells_ref[...], upper_ref, lower_ref)
    copies = [
        pltpu.make_async_copy(cells_ref.at[pl.ds(k * width, width)], out_ref.at[r], sems.at[k])
        for k, r in enumerate((0, rows - 1))
    ]
    for copy in copies:
        copy.start()
    for copy in copies:
        copy.wait()


def evolved(shifted, before, after, upwind_flags, courant, upper, lower):
    rows, width, bins = shifted.shape
    step = min(64, width)
    smem, vmem = pl.BlockSpec(memory_space=pltpu.SMEM), pl.BlockSpec(memory_space=pltpu.VMEM)
    whole = lambda a: pl.BlockSpec(a.shape, lambda i: (0,) * a.ndim)
    block = pl.BlockSpec((rows, step, bins), lambda i: (0, i, 0))
    cells = (rows - 2) * width
    out = pl.pallas_call(
        interior_kernel,
        grid=(width // step,),
        out_shape=jax.ShapeDtypeStruct(shifted.shape, shifted.dtype),
        in_specs=[smem, block, whole(courant), whole(upper), whole(lower)],
        out_specs=block,
        scratch_shapes=[pltpu.VMEM(((rows - 2) * step, bins), jnp.float32)],
        compiler_params=pltpu.CompilerParams(vmem_limit_bytes=40 * MIB),
        cost_estimate=pl.CostEstimate(
            flops=2 * cells * (upper.size + lower.size), bytes_accessed=8 * shifted.size, transcendentals=0
        ),
        name="interior",
    )(upwind_flags, shifted, courant, upper, lower)
    pair = lambda at: pl.BlockSpec((2, width, bins), lambda i: (at, 0, 0))
    return pl.pallas_call(
        ends_kernel,
        grid=(1,),
        out_shape=jax.ShapeDtypeStruct(shifted.shape, shifted.dtype),
        in_specs=[
            smem, pair(0), pair(rows // 2 - 1), whole(before), whole(after), whole(courant), whole(upper), whole(lower),
            pl.BlockSpec(memory_space=pl.ANY),
        ],
        out_specs=pl.BlockSpec(memory_space=pl.ANY),
        scratch_shapes=[pltpu.VMEM((2 * width, bins), jnp.float32), pltpu.SemaphoreType.DMA((2,))],
        input_output_aliases={8: 0},
        compiler_params=pltpu.CompilerParams(vmem_limit_bytes=24 * MIB),
        name="ends",
    )(upwind_flags, shifted, shifted, before, after, courant, upper, lower, out)


def shards(density, shift_cells, upwind_flags, courant, gain_factors, rate_left, rate_right):
    rows, width, bins = density.shape
    ring, bands = lax.axis_size("azi"), lax.axis_size("rad")
    row = lax.all_to_all(density, "azi", 0, 0, tiled=True)
    shift = lax.dynamic_slice(shift_cells, (lax.axis_index("azi"),), (1,))
    row = rolled(row.reshape(ring * width, bins), shift)
    shifted = lax.all_to_all(row.reshape(ring, width, bins), "azi", 0, 0, tiled=True)
    up = [(i, i + 1) for i in range(bands - 1)]
    before = lax.ppermute(shifted[rows - 1 :], "rad", up)
    after = lax.ppermute(shifted[:1], "rad", [(j, i) for i, j in up])
    upper, lower = weights(gain_factors, rate_left, rate_right)
    return evolved(shifted, before, after, upwind_flags, courant, upper, lower)


def solution(mesh):
    return jax.shard_map(
        shards,
        mesh=mesh,
        in_specs=(P("rad", "azi", None), P("rad"), P("rad"), P("rad", None), P(), P(), P()),
        out_specs=P("rad", "azi", None),
        check_vma=False,
    )
```

time: 244 us -> 240 us (0.984)
  waiting for transfers between devices: 192 us -> 185 us
  Pallas kernels: 18.9 us -> 21.4 us
    ppermute x1, waiting for transfers between devices: 5.71 us -> 0.01 us  [shards(): before = lax.ppermute(shifted[rows - 1:], 'rad', up)]
    pallas_call x1 -> x3, Pallas kernels: 16 us -> 18.3 us  [the longest x1 13.4 us: evolved(): pl.pallas_call(interior_kernel, grid=(width // step,), out_shape=jax.Shap...]
  transfers between devices with their start and end apart: 4 -> 4, of which waited for: 4 -> 2; matrix products, arithmetic and copies ran while one was open for 1% -> 0% of each run, Pallas kernels for 0% -> 7%
where the time goes in v2:
time: 240 us; the launch traced here: 238 us
  waiting for transfers between devices  185 us (77%)
  starting transfers between devices  25.9 us (11%)
  Pallas kernels  21.4 us (9%)
  local copies, waits for them, and re-layouts  5.6 us (2%)
    all_to_all x1, waiting for transfers between devices, shards(): row = lax.all_to_all(density, 'azi', 0, 0, tiled=True)  93.1 us
    all_to_all x1, waiting for transfers between devices, shards(): lax.all_to_all(row.reshape(ring, width, bins), 'azi', 0, 0, tiled=True)  91.6 us
    pallas_call x1, Pallas kernels, evolved(): pl.pallas_call(interior_kernel, grid=(width // step,), out_shape=jax.Shap...  13.4 us
    all_to_all x1, starting transfers between devices, shards(): row = lax.all_to_all(density, 'azi', 0, 0, tiled=True)  9.84 us
    all_to_all x1, starting transfers between devices, shards(): lax.all_to_all(row.reshape(ring, width, bins), 'azi', 0, 0, tiled=True)  8.67 us
  transfers between devices with their start and end apart: 4, of which 2 were waited for; matrix products, arithmetic and copies ran while one was open for 0% of the time, Pallas kernels for 7%

profile of v2, /device:TPU:56, one launch (start us, length us, event | category | flops | bytes accessed | tf_op | source)
XLA Modules:
  0.0 237.7 jit_solution(9309825449367313844)
XLA Ops:
  0.0 0.0 copy-start.5
  0.0 9.8 %all-to-all-start = ((f32[32,256,128]{2,1,0:T(8,128)}), f32[32,256,128]{2,1,0:T(8,128)}, u32[]{:S(2)}, u32[]{:S(2)}) async-start(f32[32,256,128]{2,1,0:T(8,128)} %param.7), calls=%async_computation | async-start | bytes 8388608 | tf_op jit(solution)/shard_map/all_to_all | solution.py:184
  9.9 0.0 copy-done.5
  9.9 0.6 dynamic_slice.3.shift_ref
  10.5 93.1 %all-to-all-done = f32[32,256,128]{2,1,0:T(8,128)} async-done(((f32[32,256,128]{2,1,0:T(8,128)}), f32[32,256,128]{2,1,0:T(8,128)}, u32[]{:S(2)}, u32[]{:S(2)}) %all-to-all-start) | async-done | bytes 4194336 | tf_op jit(solution)/shard_map/all_to_all | solution.py:184
  103.6 3.0 %roll.1 = f32[8192,1,128]{2,1,0:T(1,128)S(1)} custom-call(s32[1]{0:T(128)} %dynamic_slice.3.shift_ref, f32[8192,1,128]{2,1,0:T(1,128)} %bitcast.row_ref), custom_call_target="tpu_custom_call" | custom-call | bytes 8388608 | tf_op jit(solution)/shard_map/roll/pallas_call | solution.py:39
  106.6 0.0 copy-start
  106.7 2.0 copy-done
  108.7 0.0 copy-start.3
  108.7 0.0 copy-start.4
  108.7 8.7 %all-to-all-start.1 = ((f32[32,256,128]{2,1,0:T(8,128)}), f32[32,256,128]{2,1,0:T(8,128)}, u32[]{:S(2)}, u32[]{:S(2)}) async-start(f32[32,256,128]{2,1,0:T(8,128)} %bitcast.2), calls=%async_computation.1 | async-start | bytes 8388608 | tf_op jit(solution)/shard_map/all_to_all | solution.py:187
  117.3 2.1 weights.1
  119.5 91.6 %all-to-all-done.1.x_ref.low_ref.high_ref = f32[32,256,128]{2,1,0:T(8,128)} async-done(((f32[32,256,128]{2,1,0:T(8,128)}), f32[32,256,128]{2,1,0:T(8,128)}, u32[]{:S(2)}, u32[]{:S(2)}) %all-to-all-start.1) | async-done | bytes 4194336 | tf_op jit(solution)/shard_map/all_to_all | solution.py:187
  211.1 1.0 fusion
  212.1 4.5 %collective-permute-start.1 = (f32[1,256,128]{2,1,0:T(8,128)S(1)}, f32[1,256,128]{2,1,0:T(8,128)S(1)}, u32[]{:S(2)}, u32[]{:S(2)}) collective-permute-start(f32[1,256,128]{2,1,0:T(8,128)S(1)} %get-tuple-element.9), channel_id=1, source_target_pairs={{32,0},{64,32},{96,64},{128,96},{160,128},{192,160},{224,192},{33,... | collective-permute-start | bytes 393224 | tf_op jit(solution)/shard_map/ppermute | solution.py:190
  216.6 2.9 %collective-permute-start = (f32[1,256,128]{2,1,0:T(8,128)S(1)}, f32[1,256,128]{2,1,0:T(8,128)S(1)}, u32[]{:S(2)}, u32[]{:S(2)}) collective-permute-start(f32[1,256,128]{2,1,0:T(8,128)S(1)} %get-tuple-element.10), channel_id=1, source_target_pairs={{0,32},{32,64},{64,96},{96,128},{128,160},{160,192},{192,224},{1,3... | collective-permute-start | bytes 393224 | tf_op jit(solution)/shard_map/ppermute | solution.py:189
  219.4 0.0 copy-done.3
  219.4 0.0 copy-done.4
  219.4 0.0 copy-start.1
  219.5 1.1 copy-done.1
  220.5 0.0 copy-start.2
  220.5 0.9 copy-done.2
  221.5 13.4 %interior.1.kept_ref = f32[32,256,128]{2,1,0:T(8,128)} custom-call(s32[32]{0:T(128)S(1)} %copy-done.4, f32[32,256,128]{2,1,0:T(8,128)} %all-to-all-done.1.x_ref.low_ref.high_ref, f32[32,128]{1,0:T(8,128)S(1)} %copy-done.3, bf16[256,1152]{1,0:T(8,128)(2,1)S(1)} %copy-done.1, bf16[128,1024]{1,0:T(8,128)(2,1)S(1)} %copy-done.2), custom_call_target="tpu_custom_call" | custom-call | flops 6543114240 | bytes 8388608 | tf_op jit(solution)/shard_map/interior/pallas_call | solution.py:151
  234.9 0.0 collective-permute-done.1.after_ref
  234.9 0.0 collective-permute-done.before_ref
  234.9 2.8 %ends.1 = f32[32,256,128]{2,1,0:T(8,128)} custom-call(s32[32]{0:T(128)S(1)} %copy-done.4, f32[32,256,128]{2,1,0:T(8,128)} %all-to-all-done.1.x_ref.low_ref.high_ref, f32[32,256,128]{2,1,0:T(8,128)} %all-to-all-done.1.x_ref.low_ref.high_ref, f32[1,256,128]{2,1,0:T(8,128)S(1)} %collective-permute-done.before_ref, ...), custom_call_target="tpu_custom_call", output_to_operand_aliasing={{}: (8, {})} | custom-call | tf_op jit(solution)/shard_map/ends/pallas_call | solution.py:165
Async XLA Ops:
  0.0 9.9 %copy-start.5 = (s32[32]{0:T(128)S(1)}, s32[32]{0:T(128)}, u32[]{:S(2)}) copy-start(s32[32]{0:T(128)} %param.8) | copy-start | bytes 388
  0.0 103.6 %all-to-all-start = ((f32[32,256,128]{2,1,0:T(8,128)}), f32[32,256,128]{2,1,0:T(8,128)}, u32[]{:S(2)}, u32[]{:S(2)}) async-start(f32[32,256,128]{2,1,0:T(8,128)} %param.7), calls=%async_computation | async-start | bytes 8388608 | tf_op jit(solution)/shard_map/all_to_all | solution.py:184
  106.6 2.0 copy-start
  108.7 110.8 %copy-start.3 = (f32[32,128]{1,0:T(8,128)S(1)}, f32[32,128]{1,0:T(8,128)}, u32[]{:S(2)}) copy-start(f32[32,128]{1,0:T(8,128)} %courant_ref.3) | copy-start | bytes 49156
  108.7 110.8 %copy-start.4 = (s32[32]{0:T(128)S(1)}, s32[32]{0:T(128)}, u32[]{:S(2)}) copy-start(s32[32]{0:T(128)} %flags_ref.3) | copy-start | bytes 388
  108.7 102.4 %all-to-all-start.1 = ((f32[32,256,128]{2,1,0:T(8,128)}), f32[32,256,128]{2,1,0:T(8,128)}, u32[]{:S(2)}, u32[]{:S(2)}) async-start(f32[32,256,128]{2,1,0:T(8,128)} %bitcast.2), calls=%async_computation.1 | async-start | bytes 8388608 | tf_op jit(solution)/shard_map/all_to_all | solution.py:187
  212.1 22.8 %collective-permute-start.1 = (f32[1,256,128]{2,1,0:T(8,128)S(1)}, f32[1,256,128]{2,1,0:T(8,128)S(1)}, u32[]{:S(2)}, u32[]{:S(2)}) collective-permute-start(f32[1,256,128]{2,1,0:T(8,128)S(1)} %get-tuple-element.9), channel_id=1, source_target_pairs={{32,0},{64,32},{96,64},{128,96},{160,128},{192,160},{224,192},{33,... | collective-permute-start | bytes 393224 | tf_op jit(solution)/shard_map/ppermute | solution.py:190
  216.6 18.3 %collective-permute-start = (f32[1,256,128]{2,1,0:T(8,128)S(1)}, f32[1,256,128]{2,1,0:T(8,128)S(1)}, u32[]{:S(2)}, u32[]{:S(2)}) collective-permute-start(f32[1,256,128]{2,1,0:T(8,128)S(1)} %get-tuple-element.10), channel_id=1, source_target_pairs={{0,32},{32,64},{64,96},{96,128},{128,160},{160,192},{192,224},{1,3... | collective-permute-start | bytes 393224 | tf_op jit(solution)/shard_map/ppermute | solution.py:189
  219.4 1.1 copy-start.1
  220.5 0.9 copy-start.2

commit v3 on v2

--- a/solution.py
+++ b/solution.py
@@ -35,7 +35,7 @@
 
 def rolled(row, shift):
     cells, bins = row.shape
-    parts = 2
+    parts = 4
     out = pl.pallas_call(
         roll_kernel,
         out_shape=jax.ShapeDtypeStruct((cells, 1, bins), row.dtype),
@@ -46,7 +46,7 @@
             pltpu.SemaphoreType.DMA((parts,)),
             pltpu.SemaphoreType.DMA,
         ],
-        compiler_params=pltpu.CompilerParams(vmem_limit_bytes=16 * MIB),
+        compiler_params=pltpu.CompilerParams(vmem_limit_bytes=60 * MIB),
         cost_estimate=pl.CostEstimate(flops=0, bytes_accessed=8 * cells * bins, transcendentals=0),
         name="roll",
     )(shift, row.reshape(cells, 1, bins))
@@ -123,13 +123,16 @@
     out_ref[1 : rows - 1] = result.reshape(rows - 2, width, bins)
 
 
-def ends_kernel(flags_ref, low_ref, high_ref, before_ref, after_ref, courant_ref, upper_ref, lower_ref, kept_ref,
+def ends_kernel(odd_ref, flags_ref, low_ref, high_ref, first_ref, second_ref, courant_ref, upper_ref, lower_ref, kept_ref,
                 out_ref, cells_ref, sems):
     del kept_ref
     width = low_ref.shape[1]
     rows = flags_ref.shape[0]
-    cells_ref[:width, :] = drifted(low_ref[0], low_ref[1], before_ref[0], flags_ref[0], courant_ref[:1, :])
-    cells_ref[width:, :] = drifted(high_ref[1], after_ref[0], high_ref[0], flags_ref[rows - 1], courant_ref[rows - 1 :, :])
+    odd = odd_ref[0] == 1
+    before = jnp.where(odd, first_ref[0], second_ref[0])
+    after = jnp.where(odd, second_ref[0], first_ref[0])
+    cells_ref[:width, :] = drifted(low_ref[0], low_ref[1], before, flags_ref[0], courant_ref[:1, :])
+    cells_ref[width:, :] = drifted(high_ref[1], after, high_ref[0], flags_ref[rows - 1], courant_ref[rows - 1 :, :])
     cells_ref[...] = coagulated(cells_ref[...], upper_ref, lower_ref)
     copies = [
         pltpu.make_async_copy(cells_ref.at[pl.ds(k * width, width)], out_ref.at[r], sems.at[k])
@@ -141,7 +144,7 @@
         copy.wait()
 
 
-def evolved(shifted, before, after, upwind_flags, courant, upper, lower):
+def evolved(shifted, odd, first, second, upwind_flags, courant, upper, lower):
     rows, width, bins = shifted.shape
     step = min(64, width)
     smem, vmem = pl.BlockSpec(memory_space=pltpu.SMEM), pl.BlockSpec(memory_space=pltpu.VMEM)
@@ -155,7 +158,7 @@
         in_specs=[smem, block, whole(courant), whole(upper), whole(lower)],
         out_specs=block,
         scratch_shapes=[pltpu.VMEM(((rows - 2) * step, bins), jnp.float32)],
-        compiler_params=pltpu.CompilerParams(vmem_limit_bytes=40 * MIB),
+        compiler_params=pltpu.CompilerParams(vmem_limit_bytes=60 * MIB),
         cost_estimate=pl.CostEstimate(
             flops=2 * cells * (upper.size + lower.size), bytes_accessed=8 * shifted.size, transcendentals=0
         ),
@@ -167,15 +170,15 @@
         grid=(1,),
         out_shape=jax.ShapeDtypeStruct(shifted.shape, shifted.dtype),
         in_specs=[
-            smem, pair(0), pair(rows // 2 - 1), whole(before), whole(after), whole(courant), whole(upper), whole(lower),
+            smem, smem, pair(0), pair(rows // 2 - 1), whole(first), whole(second), whole(courant), whole(upper), whole(lower),
             pl.BlockSpec(memory_space=pl.ANY),
         ],
         out_specs=pl.BlockSpec(memory_space=pl.ANY),
         scratch_shapes=[pltpu.VMEM((2 * width, bins), jnp.float32), pltpu.SemaphoreType.DMA((2,))],
-        input_output_aliases={8: 0},
+        input_output_aliases={9: 0},
         compiler_params=pltpu.CompilerParams(vmem_limit_bytes=24 * MIB),
         name="ends",
-    )(upwind_flags, shifted, shifted, before, after, courant, upper, lower, out)
+    )(odd, upwind_flags, shifted, shifted, first, second, courant, upper, lower, out)
 
 
 def shards(density, shift_cells, upwind_flags, courant, gain_factors, rate_left, rate_right):
@@ -185,11 +188,14 @@
     shift = lax.dynamic_slice(shift_cells, (lax.axis_index("azi"),), (1,))
     row = rolled(row.reshape(ring * width, bins), shift)
     shifted = lax.all_to_all(row.reshape(ring, width, bins), "azi", 0, 0, tiled=True)
-    up = [(i, i + 1) for i in range(bands - 1)]
-    before = lax.ppermute(shifted[rows - 1 :], "rad", up)
-    after = lax.ppermute(shifted[:1], "rad", [(j, i) for i, j in up])
+    odd = lax.rem(lax.axis_index("rad"), 2)
+    top, bottom = shifted[rows - 1 :], shifted[:1]
+    swaps = []
+    for start, sent in ((0, jnp.where(odd == 1, bottom, top)), (1, jnp.where(odd == 1, top, bottom))):
+        pairs = [(i, i + 1) for i in range(start, bands - 1, 2)]
+        swaps.append(lax.ppermute(sent, "rad", pairs + [(j, i) for i, j in pairs]))
     upper, lower = weights(gain_factors, rate_left, rate_right)
-    return evolved(shifted, before, after, upwind_flags, courant, upper, lower)
+    return evolved(shifted, odd[None], *swaps, upwind_flags, courant, upper, lower)
 
 
 def solution(mesh):

time: 240 us -> 236 us (0.983)
  local copies, waits for them, and re-layouts: 5.6 us -> 0.69 us
  starting transfers between devices: 25.9 us -> 23 us
    unnamed x12 -> x10, local copies, waits for them, and re-layouts: 4.03 us -> 0.02 us
    ppermute x2, starting transfers between devices: 7.35 us -> 4.93 us  [shards(): swaps.append(lax.ppermute(sent, 'rad', pairs + [(j, i) for i, j in pairs]))]
where the time goes in v3:
time: 236 us; the launch traced here: 232 us
  waiting for transfers between devices  185 us (78%)
  starting transfers between devices  23 us (10%)
  Pallas kernels  22.7 us (10%)
    all_to_all x1, waiting for transfers between devices, shards(): row = lax.all_to_all(density, 'azi', 0, 0, tiled=True)  93 us
    all_to_all x1, waiting for transfers between devices, shards(): lax.all_to_all(row.reshape(ring, width, bins), 'azi', 0, 0, tiled=True)  91.6 us
    pallas_call x1, Pallas kernels, evolved(): pl.pallas_call(interior_kernel, grid=(width // step,), out_shape=jax.Shap...  13.9 us
    all_to_all x1, starting transfers between devices, shards(): row = lax.all_to_all(density, 'azi', 0, 0, tiled=True)  9.84 us
    all_to_all x1, starting transfers between devices, shards(): lax.all_to_all(row.reshape(ring, width, bins), 'azi', 0, 0, tiled=True)  8.19 us
    ppermute x2, starting transfers between devices, shards(): swaps.append(lax.ppermute(sent, 'rad', pairs + [(j, i) for i, j in pairs]))  4.93 us
  transfers between devices with their start and end apart: 4, of which 2 were waited for; matrix products, arithmetic and copies ran while one was open for 0% of the time, Pallas kernels for 7%

profile of v3, /device:TPU:56, one launch (start us, length us, event | category | flops | bytes accessed | tf_op | source)
XLA Modules:
  0.0 232.1 jit_solution(13838075928083579397)
XLA Ops:
  0.0 0.0 copy-start.4
  0.0 9.8 %all-to-all-start = ((f32[32,256,128]{2,1,0:T(8,128)}), f32[32,256,128]{2,1,0:T(8,128)}, u32[]{:S(2)}, u32[]{:S(2)}) async-start(f32[32,256,128]{2,1,0:T(8,128)} %param.7), calls=%async_computation | async-start | bytes 8388608 | tf_op jit(solution)/shard_map/all_to_all | solution.py:187
  9.9 0.0 copy-done.4
  9.9 0.7 dynamic_slice.3.shift_ref
  10.5 93.0 %all-to-all-done = f32[32,256,128]{2,1,0:T(8,128)} async-done(((f32[32,256,128]{2,1,0:T(8,128)}), f32[32,256,128]{2,1,0:T(8,128)}, u32[]{:S(2)}, u32[]{:S(2)}) %all-to-all-start) | async-done | bytes 4194336 | tf_op jit(solution)/shard_map/all_to_all | solution.py:187
  103.6 4.0 %roll.1 = f32[8192,1,128]{2,1,0:T(1,128)} custom-call(s32[1]{0:T(128)} %dynamic_slice.3.shift_ref, f32[8192,1,128]{2,1,0:T(1,128)} %bitcast.1.row_ref), custom_call_target="tpu_custom_call" | custom-call | bytes 8388608 | tf_op jit(solution)/shard_map/roll/pallas_call | solution.py:39
  107.6 8.2 %all-to-all-start.1 = ((f32[32,256,128]{2,1,0:T(8,128)}), f32[32,256,128]{2,1,0:T(8,128)}, u32[]{:S(2)}, u32[]{:S(2)}) async-start(f32[32,256,128]{2,1,0:T(8,128)} %bitcast.3), calls=%async_computation.1 | async-start | bytes 8388608 | tf_op jit(solution)/shard_map/all_to_all | solution.py:190
  115.8 2.2 weights.1
  117.9 91.6 %all-to-all-done.1.x_ref.low_ref.high_ref = f32[32,256,128]{2,1,0:T(8,128)} async-done(((f32[32,256,128]{2,1,0:T(8,128)}), f32[32,256,128]{2,1,0:T(8,128)}, u32[]{:S(2)}, u32[]{:S(2)}) %all-to-all-start.1) | async-done | bytes 4194336 | tf_op jit(solution)/shard_map/all_to_all | solution.py:190
  209.5 1.0 slice_select_fusion
  210.5 4.8 %collective-permute-start.1 = (f32[1,256,128]{2,1,0:T(8,128)S(1)}, f32[1,256,128]{2,1,0:T(8,128)S(1)}, u32[]{:S(2)}, u32[]{:S(2)}) collective-permute-start(f32[1,256,128]{2,1,0:T(8,128)S(1)} %get-tuple-element.9), channel_id=1, source_target_pairs={{32,64},{96,128},{160,192},{64,32},{128,96},{192,160},{33,65},{97,... | collective-permute-start | bytes 393224 | tf_op jit(solution)/shard_map/ppermute | solution.py:196
  215.3 0.1 collective-permute-start
  215.4 0.0 copy-start
  215.4 0.0 copy-start.1
  215.4 0.0 copy-start.2
  215.5 0.0 copy-start.3
  215.5 13.9 %interior.1.kept_ref = f32[32,256,128]{2,1,0:T(8,128)} custom-call(s32[32]{0:T(128)} %flags_ref.3, f32[32,256,128]{2,1,0:T(8,128)} %all-to-all-done.1.x_ref.low_ref.high_ref, f32[32,128]{1,0:T(8,128)} %courant_ref.3, bf16[256,1152]{1,0:T(8,128)(2,1)} %get-tuple-element.7.upper_ref, bf16[128,1024]{1,0:T(8,128)(2,1)} %get-tuple-element.8.lower_ref), custom_call_target="tpu_custom_call" | custom-call | flops 6543114240 | bytes 8388608 | tf_op jit(solution)/shard_map/interior/pallas_call | solution.py:154
  229.3 0.0 collective-permute-done.1.second_ref
  229.3 0.0 collective-permute-done.first_ref
  229.3 0.0 copy-done
  229.3 0.0 copy-done.1
  229.4 0.0 copy-done.2
  229.4 0.0 copy-done.3
  229.4 2.7 %ends.1 = f32[32,256,128]{2,1,0:T(8,128)} custom-call(s32[1]{0:T(128)} %bitcast.odd_ref, s32[32]{0:T(128)S(1)} %copy-done.3, f32[32,256,128]{2,1,0:T(8,128)} %all-to-all-done.1.x_ref.low_ref.high_ref, f32[32,256,128]{2,1,0:T(8,128)} %all-to-all-done.1.x_ref.low_ref.high_ref, ...), custom_call_target="tpu_custom_call", output_to_operand_aliasing={{}: (9, {})} | custom-call | tf_op jit(solution)/shard_map/ends/pallas_call | solution.py:168
Async XLA Ops:
  0.0 9.9 %copy-start.4 = (s32[32]{0:T(128)S(1)}, s32[32]{0:T(128)}, u32[]{:S(2)}) copy-start(s32[32]{0:T(128)} %param.8) | copy-start | bytes 388
  0.0 103.6 %all-to-all-start = ((f32[32,256,128]{2,1,0:T(8,128)}), f32[32,256,128]{2,1,0:T(8,128)}, u32[]{:S(2)}, u32[]{:S(2)}) async-start(f32[32,256,128]{2,1,0:T(8,128)} %param.7), calls=%async_computation | async-start | bytes 8388608 | tf_op jit(solution)/shard_map/all_to_all | solution.py:187
  107.6 101.9 %all-to-all-start.1 = ((f32[32,256,128]{2,1,0:T(8,128)}), f32[32,256,128]{2,1,0:T(8,128)}, u32[]{:S(2)}, u32[]{:S(2)}) async-start(f32[32,256,128]{2,1,0:T(8,128)} %bitcast.3), calls=%async_computation.1 | async-start | bytes 8388608 | tf_op jit(solution)/shard_map/all_to_all | solution.py:190
  210.5 18.9 %collective-permute-start.1 = (f32[1,256,128]{2,1,0:T(8,128)S(1)}, f32[1,256,128]{2,1,0:T(8,128)S(1)}, u32[]{:S(2)}, u32[]{:S(2)}) collective-permute-start(f32[1,256,128]{2,1,0:T(8,128)S(1)} %get-tuple-element.9), channel_id=1, source_target_pairs={{32,64},{96,128},{160,192},{64,32},{128,96},{192,160},{33,65},{97,... | collective-permute-start | bytes 393224 | tf_op jit(solution)/shard_map/ppermute | solution.py:196
  215.3 14.0 %collective-permute-start = (f32[1,256,128]{2,1,0:T(8,128)S(1)}, f32[1,256,128]{2,1,0:T(8,128)S(1)}, u32[]{:S(2)}, u32[]{:S(2)}) collective-permute-start(f32[1,256,128]{2,1,0:T(8,128)S(1)} %get-tuple-element.10), channel_id=1, source_target_pairs={{0,32},{64,96},{128,160},{192,224},{32,0},{96,64},{160,128},{224,1... | collective-permute-start | bytes 393224 | tf_op jit(solution)/shard_map/ppermute | solution.py:196
  215.4 13.9 %copy-start = (bf16[256,1152]{1,0:T(8,128)(2,1)S(1)}, bf16[256,1152]{1,0:T(8,128)(2,1)}, u32[]{:S(2)}) copy-start(bf16[256,1152]{1,0:T(8,128)(2,1)} %get-tuple-element.7.upper_ref) | copy-start | bytes 1769476
  215.4 13.9 %copy-start.1 = (bf16[128,1024]{1,0:T(8,128)(2,1)S(1)}, bf16[128,1024]{1,0:T(8,128)(2,1)}, u32[]{:S(2)}) copy-start(bf16[128,1024]{1,0:T(8,128)(2,1)} %get-tuple-element.8.lower_ref) | copy-start | bytes 786436
  215.4 13.9 %copy-start.2 = (f32[32,128]{1,0:T(8,128)S(1)}, f32[32,128]{1,0:T(8,128)}, u32[]{:S(2)}) copy-start(f32[32,128]{1,0:T(8,128)} %courant_ref.3) | copy-start | bytes 49156
  215.5 13.9 %copy-start.3 = (s32[32]{0:T(128)S(1)}, s32[32]{0:T(128)}, u32[]{:S(2)}) copy-start(s32[32]{0:T(128)} %flags_ref.3) | copy-start | bytes 388
